TPU v7x, 128 devices: a whole 4x4x4 slice. The times are simulated.
128 devices in a mesh: row: 8 (over y_lo, z), col: 16 (over y_hi, x, core).
Axes of the slice: x: 4, y: 4 (y_hi: 2, y_lo: 2; y = y_hi * 2 + y_lo), z: 4, core: 2. Of those that a mesh axis runs over, the one named last changes fastest.
Arguments:
- ocean_state: float32 [1024, 24, 4096], P('row', None, 'col'), may hold values from -6 to 6
- saved_checksums: float32 [1024, 4, 24, 256], P(('row', 'col')), may hold values from -24 to 24
- checksum_weights: int32 [4, 16], replicated, may hold values from 1 to 3
- failed_devices: int32 [8, 2], replicated, may hold values from 0 to 15, as said below
- column_op: float32 [24, 24], replicated, may hold values from -1.25 to 1.25
- diffusivity: float32 [24], replicated, may hold values from 0.04 to 0.2
Outputs:
- stepped_state: float32 [1024, 24, 4096], P('row', None, 'col')
- fresh_parity: float32 [1024, 4, 24, 256], P(('row', 'col'))
Inputs may be any that keep to these rules, and one draw needn't show every extreme that they name: `failed_devices`: the two entries of a row differ.
All inputs are finite; a program needn't handle non-finite values.
Results may differ from a plain program's by a relative error of at most 0.00022.
Values sent between devices are 32-bit elements; how exact they have to be, the bound alone decides.
No kernel may reach another device: no remote copies, remote signals or barrier semaphores. Data moves between devices by JAX's collectives and lax.ppermute only.
A program may use at most 64 MiB of HBM per device.

v0:
```python
import jax
import jax.numpy as jnp
from jax import lax
from jax.sharding import PartitionSpec as P


def with_halo(cells, sides, width):
    for axis, dim in sides:
        count = lax.axis_size(axis)
        ends = count - 1
        head = lax.slice_in_dim(cells, 0, width, axis=dim)
        tail = lax.slice_in_dim(cells, cells.shape[dim] - width, cells.shape[dim], axis=dim)
        cells = jnp.concatenate(
            [
                lax.ppermute(tail, axis, [(i, (i + 1) % count) for i in range(ends)]),
                cells,
                lax.ppermute(head, axis, [((i + 1) % count, i) for i in range(ends)]),
            ],
            axis=dim,
        )
    return cells


def weighted(block, weight_vec):
    return block[:, None, :, :] * weight_vec[None, :, None, None]


def per_device(
    ocean_state, saved_checksums, checksum_weights, failed_devices, column_op, diffusivity
):
    my_col = lax.axis_index("col")
    my_row = lax.axis_index("row")
    lost_pair = lax.dynamic_index_in_dim(failed_devices, my_row, 0, keepdims=False)
    lost_a = lost_pair[0]
    lost_b = lost_pair[1]
    float_weights = checksum_weights.astype(jnp.float32)
    weight_a = jnp.take(float_weights, lost_a, axis=1)
    weight_b = jnp.take(float_weights, lost_b, axis=1)
    own_weight = jnp.take(float_weights, my_col, axis=1)
    is_lost = (my_col == lost_a) | (my_col == lost_b)
    survive = jnp.where(is_lost, 0.0, 1.0).astype(jnp.float32)
    living_devices = lax.psum_scatter(
        weighted(ocean_state, own_weight * survive), "col", scatter_dimension=0, tiled=True
    )
    remaining_sum = saved_checksums - living_devices
    gram_aa = jnp.sum(weight_a * weight_a) + 1.0
    gram_bb = jnp.sum(weight_b * weight_b) + 1.0
    gram_ab = jnp.sum(weight_a * weight_b)
    determinant = gram_aa * gram_bb - gram_ab * gram_ab
    coeff_a = (gram_bb * weight_a - gram_ab * weight_b) / determinant
    coeff_b = (gram_aa * weight_b - gram_ab * weight_a) / determinant
    rebuilt_a = jnp.sum(remaining_sum * coeff_a[None, :, None, None], axis=1)
    rebuilt_b = jnp.sum(remaining_sum * coeff_b[None, :, None, None], axis=1)
    both_rebuilt = jnp.stack((rebuilt_a, rebuilt_b), axis=1)
    gathered = lax.all_gather(both_rebuilt, "col", axis=0, tiled=True)
    chosen = jnp.where(my_col == lost_a, gathered[:, 0], gathered[:, 1])
    recovered = jnp.where(is_lost, chosen, ocean_state)
    fresh_parity = lax.psum_scatter(
        weighted(recovered, own_weight), "col", scatter_dimension=0, tiled=True
    )
    mixed_state = recovered + jnp.tanh(
        jnp.einsum("gf,xfy->xgy", column_op, recovered, precision=lax.Precision.HIGHEST)
    )
    padded = with_halo(mixed_state, (("row", 0), ("col", 2)), 1)
    laplace_term = (
        padded[2:, :, 1:-1]
        + padded[:-2, :, 1:-1]
        + padded[1:-1, :, 2:]
        + padded[1:-1, :, :-2]
        - 4.0 * mixed_state
    )
    stepped_state = mixed_state + diffusivity[None, :, None] * laplace_term
    return (stepped_state, fresh_parity)


def solution(mesh):
    return jax.shard_map(
        per_device,
        mesh=mesh,
        in_specs=(P("row", None, "col"), P(("row", "col"), None, None, None), P(), P(), P(), P()),
        out_specs=(P("row", None, "col"), P(("row", "col"), None, None, None)),
        check_vma=False,
    )
```

profile of v0, /device:TPU:15, one launch (start us, length us, event | category | flops | bytes accessed | tf_op | source)
XLA Modules:
  0.0 349.6 jit_solution(15614936949558506778)
XLA Ops:
  7.2 0.0 reduce-scatter.3.cloned.1.call-start
  7.2 0.8 constant_dynamic-slice_fusion
  8.0 0.5 fusion.11
  13.7 0.7 convert_element_type.3
  14.4 0.2 select_reduce_fusion.2
  14.6 8.5 %broadcast_multiply_fusion.1 = f32[128,4,24,256]{3,2,1,0:T(8,128)} fusion(f32[4]{0:T(128)S(1)} %broadcast_multiply_fusion.2, f32[128,24,256]{2,1,0:T(8,128)} %param.8), kind=kLoop, calls=%fused_computation.1 | loop fusion | flops 3145728 | bytes 15728656 | tf_op jit(solution)/shard_map/mul | solution.py:25
  23.1 0.0 all-gather.2.cloned.1.call-start
  23.2 0.7 multiply_reduce_fusion.3
  26.7 0.7 subtract_divide_fusion
  27.3 117.1 %reduce-scatter.3.cloned.1.call-done = f32[8,4,24,256]{3,2,1,0:T(8,128)} async-done(((f32[128,4,24,256]{3,2,1,0:T(8,128)}), f32[8,4,24,256]{3,2,1,0:T(8,128)}) %reduce-scatter.3.cloned.1.call-update) | async-done | bytes 786448 | tf_op jit(solution)/shard_map/reduce_scatter | solution.py:42
  144.5 1.6 multiply_reduce_fusion.1
  146.1 0.8 pad_maximum_fusion.9
  146.9 0.0 all-gather.2.cloned.1.call-update
  146.9 0.0 reduce-scatter.5.cloned.1.call-start
  146.9 65.6 %all-gather.2.cloned.1.call-done = f32[128,2,24,256]{3,2,0,1:T(8,128)} async-done(((f32[8,2,24,256]{3,2,0,1:T(8,128)}), f32[128,2,24,256]{3,2,0,1:T(8,128)}) %all-gather.2.cloned.1.call-update) | async-done | bytes 6291472 | tf_op jit(solution)/shard_map/all_gather | solution.py:55
  212.5 3.7 %fusion.7 = f32[128,24,256]{2,1,0:T(8,128)S(1)} fusion(f32[128,24,256]{2,1,0:T(8,128)S(1)} %copy-done.2, f32[128,2,24,256]{3,2,0,1:T(8,128)} %all-gather.2.cloned.1.call-done, pred[]{:T(512)S(6)} %eq.7, pred[]{:T(512)S(6)} %or.3), kind=kLoop, calls=%fused_computation.19 | loop fusion | flops 1572864 | bytes 12582914 | tf_op jit(solution)/shard_map/jit(_where)/select_n | solution.py:57
  216.2 1.7 copy-done.1
  217.8 6.5 %broadcast_multiply_fusion = f32[128,4,24,256]{3,2,1,0:T(8,128)} fusion(f32[4]{0:T(128)S(1)} %get-tuple-element.16, f32[128,24,256]{2,1,0:T(8,128)S(1)} %fusion.7), kind=kLoop, calls=%fused_computation | loop fusion | flops 3145728 | bytes 15728656 | tf_op jit(solution)/shard_map/mul | solution.py:25
  224.4 5.9 %bitcast_add_fusion = f32[128,24,256]{2,1,0:T(8,128)S(1)} fusion(f32[128,24,256]{2,1,0:T(8,128)} %copy-done.1, f32[24,24]{1,0:T(8,128)S(1)} %copy-done), kind=kOutput, calls=%fused_computation.20 | convolution fusion | flops 227278848 | bytes 6293760 | tf_op jit(solution)/shard_map/gf,xfy->xgy/dot_general | solution.py:62
  230.3 3.2 collective-permute-start.1
  233.5 4.2 %collective-permute-start = (f32[1,24,256]{2,1,0:T(8,128)S(1)}, f32[1,24,256]{2,1,0:T(8,128)S(1)}, u32[]{:S(2)}, u32[]{:S(2)}) collective-permute-start(f32[1,24,256]{2,1,0:T(8,128)S(1)} %get-tuple-element.25), channel_id=1, source_target_pairs={{16,0},{32,16},{48,32},{64,48},{80,64},{96,80},{112,96},{17,1},{33... | collective-permute-start | bytes 73736 | tf_op jit(solution)/shard_map/ppermute | solution.py:17
  237.7 0.9 collective-permute-done
  238.7 0.2 pad_maximum_fusion
  238.9 2.2 fusion.9
  241.0 2.6 copy.8
  243.6 3.3 collective-permute-start.2
  247.0 2.6 copy.10
  249.6 6.0 %collective-permute-start.3 = (f32[130,24,1]{0,1,2:T(8,128)S(1)}, f32[130,24,1]{0,1,2:T(8,128)S(1)}, u32[]{:S(2)}, u32[]{:S(2)}) collective-permute-start(f32[130,24,1]{0,1,2:T(8,128)S(1)} %copy.10), channel_id=1, source_target_pairs={{0,1},{1,2},{2,3},{3,4},{4,5},{5,6},{6,7},{7,8},{8,9},{9,10},{10,1... | collective-permute-start | bytes 37448 | tf_op jit(solution)/shard_map/ppermute | solution.py:15
  255.6 2.1 copy.9
  257.7 2.2 copy.11
  259.9 7.4 %fusion.3 = f32[128,24,256]{2,1,0:T(8,128)} fusion(f32[128,24,256]{2,1,0:T(8,128)S(1)} %bitcast_add_fusion, f32[130,24,1]{2,1,0:T(8,128)} %copy.11, f32[1,24,256]{2,1,0:T(8,128)S(1)} %collective-permute-done, f32[1,24,256]{2,1,0:T(8,128)S(1)} %collective-permute-done.1, f32[130,24,1]{2,1,0:T(8,128)} %copy.9, f32[24]{0:T(128)S(1)} %copy-done.3), kind=kLoop, calls=%fused_computation.7 | loop fusion | flops 11796480 | bytes 6365664 | tf_op jit(solution)/shard_map/add | solution.py:72
  267.3 75.8 %reduce-scatter.5.cloned.1.call-done = f32[8,4,24,256]{3,2,1,0:T(8,128)} async-done(((f32[128,4,24,256]{3,2,1,0:T(8,128)}), f32[8,4,24,256]{3,2,1,0:T(8,128)}) %reduce-scatter.5.cloned.1.call-update) | async-done | bytes 786448 | tf_op jit(solution)/shard_map/reduce_scatter | solution.py:58
  (14 shorter events, 0.1 us)
Async XLA Ops:
  7.2 217.2 %copy-start = (f32[24,24]{1,0:T(8,128)S(1)}, f32[24,24]{1,0:T(8,128)}, u32[]{:S(2)}) copy-start(f32[24,24]{1,0:T(8,128)} %param.12) | copy-start | bytes 6916
  7.2 137.3 %reduce-scatter.3.cloned.1.call-start = ((), (), s32[]{:S(2)}) async-start(), calls=%async_computation.2 | async-start | bytes 13369344 | tf_op jit(solution)/shard_map/reduce_scatter | solution.py:42
  23.1 189.4 %copy-start.2 = (f32[128,24,256]{2,1,0:T(8,128)S(1)}, f32[128,24,256]{2,1,0:T(8,128)}, u32[]{:S(2)}) copy-start(f32[128,24,256]{2,1,0:T(8,128)} %param.8) | copy-start | bytes 9437188
  23.1 189.4 %all-gather.2.cloned.1.call-start = ((), (), s32[]{:S(2)}) async-start(), calls=%async_computation.3 | async-start | bytes 6684672 | tf_op jit(solution)/shard_map/all_gather | solution.py:55
  146.9 196.2 %reduce-scatter.5.cloned.1.call-start = ((), (), s32[]{:S(2)}) async-start(), calls=%async_computation.4 | async-start | bytes 13369344 | tf_op jit(solution)/shard_map/reduce_scatter | solution.py:58
  216.2 1.7 copy-start.1
  230.3 7.4 %collective-permute-start.1 = (f32[1,24,256]{2,1,0:T(8,128)S(1)}, f32[1,24,256]{2,1,0:T(8,128)S(1)}, u32[]{:S(2)}, u32[]{:S(2)}) collective-permute-start(f32[1,24,256]{2,1,0:T(8,128)S(1)} %get-tuple-element.24), channel_id=1, source_target_pairs={{0,16},{16,32},{32,48},{48,64},{64,80},{80,96},{96,112},{1,17},{17... | collective-permute-start | bytes 73736 | tf_op jit(solution)/shard_map/ppermute | solution.py:15
  233.5 5.1 %collective-permute-start = (f32[1,24,256]{2,1,0:T(8,128)S(1)}, f32[1,24,256]{2,1,0:T(8,128)S(1)}, u32[]{:S(2)}, u32[]{:S(2)}) collective-permute-start(f32[1,24,256]{2,1,0:T(8,128)S(1)} %get-tuple-element.25), channel_id=1, source_target_pairs={{16,0},{32,16},{48,32},{64,48},{80,64},{96,80},{112,96},{17,1},{33... | collective-permute-start | bytes 73736 | tf_op jit(solution)/shard_map/ppermute | solution.py:17
  241.0 18.8 %copy-start.3 = (f32[24]{0:T(128)S(1)}, f32[24]{0:T(128)}, u32[]{:S(2)}) copy-start(f32[24]{0:T(128)} %param.13) | copy-start | bytes 292
  243.6 12.0 %collective-permute-start.2 = (f32[130,24,1]{0,1,2:T(8,128)S(1)}, f32[130,24,1]{0,1,2:T(8,128)S(1)}, u32[]{:S(2)}, u32[]{:S(2)}) collective-permute-start(f32[130,24,1]{0,1,2:T(8,128)S(1)} %copy.8), channel_id=1, source_target_pairs={{1,0},{2,1},{3,2},{4,3},{5,4},{6,5},{7,6},{8,7},{9,8},{10,9},{11,1... | collective-permute-start | bytes 37448 | tf_op jit(solution)/shard_map/ppermute | solution.py:17
  249.6 8.1 %collective-permute-start.3 = (f32[130,24,1]{0,1,2:T(8,128)S(1)}, f32[130,24,1]{0,1,2:T(8,128)S(1)}, u32[]{:S(2)}, u32[]{:S(2)}) collective-permute-start(f32[130,24,1]{0,1,2:T(8,128)S(1)} %copy.10), channel_id=1, source_target_pairs={{0,1},{1,2},{2,3},{3,4},{4,5},{5,6},{6,7},{7,8},{8,9},{9,10},{10,1... | collective-permute-start | bytes 37448 | tf_op jit(solution)/shard_map/ppermute | solution.py:15
Sparse Core Ops, SparseCore 0:
  23.2 121.2 reduce-scatter.2
  147.8 64.6 all-gather.1
  224.5 118.5 reduce-scatter.4
where the time goes:
time: 354 us; the launch traced here: 350 us
  waiting for transfers between devices  260 us (73%)
  other arithmetic  30.8 us (9%)
  between operations  21.9 us (6%)
  starting transfers between devices  16.9 us (5%)
  local copies, waits for them, and re-layouts  14.6 us (4%)
  matrix products  5.94 us (2%)
    reduce_scatter x1, waiting for transfers between devices, per_device(): lax.psum_scatter(weighted(ocean_state, own_weight * survive), 'col', scat...  117 us
    reduce_scatter x1, waiting for transfers between devices, per_device(): lax.psum_scatter(weighted(recovered, own_weight), 'col', scatter_dimensio...  75.8 us
    all_gather x1, waiting for transfers between devices, per_device(): gathered = lax.all_gather(both_rebuilt, 'col', axis=0, tiled=True)  65.6 us
    mul x2, other arithmetic, weighted(): return block[:, None, :, :] * weight_vec[None, :, None, None]  14.9 us
    ppermute x2, starting transfers between devices, with_halo(): lax.ppermute(tail, axis, [(i, (i + 1) % count) for i in range(ends)])  9.2 us
    ppermute x2, starting transfers between devices, with_halo(): lax.ppermute(head, axis, [((i + 1) % count, i) for i in range(ends)])  7.53 us
    add x1, other arithmetic, per_device(): stepped_state = mixed_state + diffusivity[None, :, None] * laplace_term  7.39 us
  transfers between devices with their start and end apart: 7, of which 4 were waited for; matrix products, arithmetic and copies ran while one was open for 8% of the time, Pallas kernels for 0%

commit v1 on v0

v1 whole, which is shorter than its diff:
```python
import jax
import jax.numpy as jnp
from jax import lax
from jax.sharding import PartitionSpec as P


def with_halo(cells, sides, width):
    for axis, dim in sides:
        count = lax.axis_size(axis)
        ends = count - 1
        head = lax.slice_in_dim(cells, 0, width, axis=dim)
        tail = lax.slice_in_dim(cells, cells.shape[dim] - width, cells.shape[dim], axis=dim)
        cells = jnp.concatenate(
            [
                lax.ppermute(tail, axis, [(i, (i + 1) % count) for i in range(ends)]),
                cells,
                lax.ppermute(head, axis, [((i + 1) % count, i) for i in range(ends)]),
            ],
            axis=dim,
        )
    return cells


def coefficients(float_weights, lost_a, lost_b):
    weight_a = jnp.take(float_weights, lost_a, axis=1)
    weight_b = jnp.take(float_weights, lost_b, axis=1)
    gram_aa = jnp.sum(weight_a * weight_a) + 1.0
    gram_bb = jnp.sum(weight_b * weight_b) + 1.0
    gram_ab = jnp.sum(weight_a * weight_b)
    determinant = gram_aa * gram_bb - gram_ab * gram_ab
    coeff_a = (gram_bb * weight_a - gram_ab * weight_b) / determinant
    coeff_b = (gram_aa * weight_b - gram_ab * weight_a) / determinant
    return weight_a, weight_b, coeff_a, coeff_b


def per_device(
    ocean_state, saved_checksums, checksum_weights, failed_devices, column_op, diffusivity
):
    count = lax.axis_size("col")
    my_col = lax.axis_index("col")
    my_row = lax.axis_index("row")
    lost_pair = lax.dynamic_index_in_dim(failed_devices, my_row, 0, keepdims=False)
    lost_a = lost_pair[0]
    lost_b = lost_pair[1]
    float_weights = checksum_weights.astype(jnp.float32)
    weight_a, weight_b, coeff_a, coeff_b = coefficients(float_weights, lost_a, lost_b)
    members = jnp.arange(count)
    member_a = members == lost_a
    member_b = members == lost_b
    survive_weights = jnp.where(member_a | member_b, 0.0, float_weights)

    rows, fields, columns = ocean_state.shape
    strip = rows // count
    strips = lax.all_to_all(ocean_state, "col", 0, 0, tiled=True)
    strips = strips.reshape(count, strip, fields, columns)
    living = [
        sum(survive_weights[k, c] * strips[c] for c in range(count))
        for k in range(float_weights.shape[0])
    ]
    residue = [saved_checksums[:, k] - living[k] for k in range(len(living))]
    rebuilt_a = sum(coeff_a[k] * residue[k] for k in range(len(living)))
    rebuilt_b = sum(coeff_b[k] * residue[k] for k in range(len(living)))
    fresh_parity = jnp.stack(
        [
            living[k] + weight_a[k] * rebuilt_a + weight_b[k] * rebuilt_b
            for k in range(len(living))
        ],
        axis=1,
    )
    back = jnp.where(member_a[:, None, None, None], rebuilt_a[None], rebuilt_b[None])
    chosen = lax.all_to_all(
        back.reshape(rows, fields, columns), "col", 0, 0, tiled=True
    )
    is_lost = (my_col == lost_a) | (my_col == lost_b)
    recovered = jnp.where(is_lost, chosen, ocean_state)
    mixed_state = recovered + jnp.tanh(
        jnp.einsum("gf,xfy->xgy", column_op, recovered, precision=lax.Precision.HIGHEST)
    )
    padded = with_halo(mixed_state, (("row", 0), ("col", 2)), 1)
    laplace_term = (
        padded[2:, :, 1:-1]
        + padded[:-2, :, 1:-1]
        + padded[1:-1, :, 2:]
        + padded[1:-1, :, :-2]
        - 4.0 * mixed_state
    )
    stepped_state = mixed_state + diffusivity[None, :, None] * laplace_term
    return (stepped_state, fresh_parity)


def solution(mesh):
    return jax.shard_map(
        per_device,
        mesh=mesh,
        in_specs=(P("row", None, "col"), P(("row", "col"), None, None, None), P(), P(), P(), P()),
        out_specs=(P("row", None, "col"), P(("row", "col"), None, None, None)),
        check_vma=False,
    )
```

time: 354 us -> 206 us (0.58)
  waiting for transfers between devices: 260 us -> 68 us
  other arithmetic: 30.8 us -> 68.2 us
  starting transfers between devices: 16.9 us -> 33.4 us
  between operations: 21.9 us -> 8.32 us
  local copies, waits for them, and re-layouts: 14.6 us -> 19.3 us
    reduce_scatter x2 -> x0, waiting for transfers between devices: 193 us -> none  [the longest x1 117 us: per_device(): lax.psum_scatter(weighted(ocean_state, own_weight * survive), 'col', scat...]
    all_gather x1 -> x0, waiting for transfers between devices: 65.6 us -> none  [per_device(): gathered = lax.all_gather(both_rebuilt, 'col', axis=0, tiled=True)]
    all_to_all x0 -> x2, waiting for transfers between devices: none -> 63.1 us  [the longest x1 38 us: per_device(): lax.all_to_all(back.reshape(rows, fields, columns), 'col', 0, 0, tiled=True)]
    another operation x1 -> x3, other arithmetic: 0.77 us -> 55.8 us  [per_device(): jnp.stack([living[k] + weight_a[k] * rebuilt_a + weight_b[k] * rebuilt_b...]
    all_to_all x0 -> x2, starting transfers between devices: none -> 16 us  [the longest x1 9.02 us: per_device(): lax.all_to_all(back.reshape(rows, fields, columns), 'col', 0, 0, tiled=True)]
    mul x3 -> x0, other arithmetic: 14.9 us -> none  [the longest x2 14.9 us: weighted(): return block[:, None, :, :] * weight_vec[None, :, None, None]]
    slice x1 -> x7, local copies, waits for them, and re-layouts: 0.52 us -> 4.77 us  [the longest x4 2.84 us: per_device(): survive_weights[k, c] * strips[c]]
    ppermute x2, waiting for transfers between devices: 0.92 us -> 4.96 us  [with_halo(): lax.ppermute(head, axis, [((i + 1) % count, i) for i in range(ends)])]
  transfers between devices with their start and end apart: 7 -> 6, of which waited for: 4 -> 3; matrix products, arithmetic and copies ran while one was open for 8% -> 8% of each run, Pallas kernels for 0% -> 0%
where the time goes in v1:
time: 206 us; the launch traced here: 204 us
  other arithmetic  68.2 us (33%)
  waiting for transfers between devices  68 us (33%)
  starting transfers between devices  33.4 us (16%)
  local copies, waits for them, and re-layouts  19.3 us (9%)
  between operations  8.32 us (4%)
  matrix products  7.12 us (3%)
    another operation x3, other arithmetic, per_device(): jnp.stack([living[k] + weight_a[k] * rebuilt_a + weight_b[k] * rebuilt_b...  55.8 us
    all_to_all x1, waiting for transfers between devices, per_device(): lax.all_to_all(back.reshape(rows, fields, columns), 'col', 0, 0, tiled=True)  38 us
    all_to_all x1, waiting for transfers between devices, per_device(): strips = lax.all_to_all(ocean_state, 'col', 0, 0, tiled=True)  25.1 us
    ppermute x2, starting transfers between devices, with_halo(): lax.ppermute(tail, axis, [(i, (i + 1) % count) for i in range(ends)])  10.4 us
    all_to_all x1, starting transfers between devices, per_device(): lax.all_to_all(back.reshape(rows, fields, columns), 'col', 0, 0, tiled=True)  9.02 us
    add x1, other arithmetic, per_device(): stepped_state = mixed_state + diffusivity[None, :, None] * laplace_term  7.4 us
    dot_general x1, matrix products, per_device(): jnp.einsum('gf,xfy->xgy', column_op, recovered, precision=lax.Precision.H...  7.12 us
    all_to_all x1, starting transfers between devices, per_device(): strips = lax.all_to_all(ocean_state, 'col', 0, 0, tiled=True)  6.98 us
  transfers between devices with their start and end apart: 6, of which 3 were waited for; matrix products, arithmetic and copies ran while one was open for 8% of the time, Pallas kernels for 0%

profile of v1, /device:TPU:15, one launch (start us, length us, event | category | flops | bytes accessed | tf_op | source)
XLA Modules:
  0.0 204.3 jit_solution(4937006654457309330)
XLA Ops:
  0.7 7.0 %all-to-all-start = ((f32[128,24,256]{2,1,0:T(8,128)}), f32[128,24,256]{2,1,0:T(8,128)S(1)}, u32[]{:S(2)}, u32[]{:S(2)}) async-start(f32[128,24,256]{2,1,0:T(8,128)} %param.8), calls=%async_computation | async-start | bytes 6291456 | tf_op jit(solution)/shard_map/all_to_all | solution.py:54
  7.7 0.6 fusion.15
  12.0 1.2 compare_or_fusion
  13.4 0.2 select_reduce_fusion.1
  13.6 0.6 multiply_reduce_fusion.1
  16.9 0.7 fusion.14
  17.5 0.7 fusion.16
  18.2 0.7 subtract_divide_fusion
  18.9 0.7 fusion.18
  19.6 0.7 fusion.13
  20.3 0.7 fusion.12
  21.0 0.7 fusion.11
  21.7 25.1 %all-to-all-done = f32[128,24,256]{2,1,0:T(8,128)S(1)} async-done(((f32[128,24,256]{2,1,0:T(8,128)}), f32[128,24,256]{2,1,0:T(8,128)S(1)}, u32[]{:S(2)}, u32[]{:S(2)}) %all-to-all-start) | async-done | bytes 3145760 | tf_op jit(solution)/shard_map/all_to_all | solution.py:54
  46.8 49.3 %add_bitcast_fusion.3 = (f32[8,1,24,256]{3,2,1,0:T(8,128)}, f32[8,24,256]{2,1,0:T(8,128)S(1)}, f32[8,24,256]{2,1,0:T(8,128)S(1)}, f32[8,24,256]{2,1,0:T(8,128)},...) fusion(f32[]{:T(128)} %bitcast.83, f32[]{:T(128)} %bitcast.82, f32[8,4,24,256]{3,2,1,0:T(8,128)} %param.9, f32[]{:T(128)} %bitcast.56, ...), kind=kLoop, calls=%fused_computation.27 | loop fusion | flops 7176192 | bytes 5112104 | tf_op jit(solution)/shard_map/stack | solution.py:63
  96.1 2.0 bitcast_select_fusion
  98.1 9.0 %all-to-all-start.1 = ((f32[128,24,256]{2,1,0:T(8,128)}), f32[128,24,256]{2,1,0:T(8,128)}, u32[]{:S(2)}, u32[]{:S(2)}) async-start(f32[128,24,256]{2,1,0:T(8,128)} %bitcast_select_fusion), calls=%async_computation.1 | async-start | bytes 6291456 | tf_op jit(solution)/shard_map/all_to_all | solution.py:71
  108.4 38.0 %all-to-all-done.1 = f32[128,24,256]{2,1,0:T(8,128)} async-done(((f32[128,24,256]{2,1,0:T(8,128)}), f32[128,24,256]{2,1,0:T(8,128)}, u32[]{:S(2)}, u32[]{:S(2)}) %all-to-all-start.1) | async-done | bytes 3145760 | tf_op jit(solution)/shard_map/all_to_all | solution.py:71
  146.3 7.1 %bitcast_add_fusion = f32[128,24,256]{2,1,0:T(8,128)S(1)} fusion(f32[128,24,256]{2,1,0:T(8,128)} %all-to-all-done.1, f32[128,24,256]{2,1,0:T(8,128)} %param.8, pred[]{:T(512)S(6)} %or.6, f32[24,24]{1,0:T(8,128)S(1)} %copy-done), kind=kOutput, calls=%fused_computation.15 | convolution fusion | flops 228851712 | bytes 9439489 | tf_op jit(solution)/shard_map/gf,xfy->xgy/dot_general | solution.py:77
  153.5 3.5 %collective-permute-start.1 = (f32[1,24,256]{2,1,0:T(8,128)S(1)}, f32[1,24,256]{2,1,0:T(8,128)S(1)}, u32[]{:S(2)}, u32[]{:S(2)}) collective-permute-start(f32[1,24,256]{2,1,0:T(8,128)S(1)} %get-tuple-element.27), channel_id=1, source_target_pairs={{0,16},{16,32},{32,48},{48,64},{64,80},{80,96},{96,112},{1,17},{17... | collective-permute-start | bytes 73736 | tf_op jit(solution)/shard_map/ppermute | solution.py:15
  157.0 4.8 %collective-permute-start = (f32[1,24,256]{2,1,0:T(8,128)S(1)}, f32[1,24,256]{2,1,0:T(8,128)S(1)}, u32[]{:S(2)}, u32[]{:S(2)}) collective-permute-start(f32[1,24,256]{2,1,0:T(8,128)S(1)} %get-tuple-element.28), channel_id=1, source_target_pairs={{16,0},{32,16},{48,32},{64,48},{80,64},{96,80},{112,96},{17,1},{33... | collective-permute-start | bytes 73736 | tf_op jit(solution)/shard_map/ppermute | solution.py:17
  161.9 4.6 %add_bitcast_fusion.2 = (f32[8,1,24,256]{3,2,1,0:T(8,128)}, f32[8,1,24,256]{3,2,1,0:T(8,128)}, f32[8,1,24,256]{3,2,1,0:T(8,128)}) fusion(f32[8,24,256]{2,1,0:T(8,128)S(1)} %get-tuple-element.21, f32[8,24,256]{2,1,0:T(8,128)S(1)} %copy-done.4, f32[8,24,256]{2,1,0:T(8,128)S(1)} %get-tuple-element.20, f32[]{:T(128)} %bitcast.87, f32[]{:T(128)} %bitcast.86, ...), kind=kLoop, calls=%fused_computation.26 | loop fusion | flops 589824 | bytes 1572888 | tf_op jit(solution)/shard_map/stack | solution.py:63
  166.7 0.4 copy-done.6
  167.1 2.2 %fusion.9 = (f32[130,24,1]{2,1,0:T(8,128)}, f32[130,24,1]{2,1,0:T(8,128)}) fusion(f32[130,24,256]{2,1,0:T(8,128)S(1)} %pad_maximum_fusion), kind=kLoop, calls=%fused_computation.46 | loop fusion | bytes 49920 | tf_op jit(solution)/shard_map/slice | solution.py:11
  169.3 3.0 %copy.26 = f32[130,24,1]{0,1,2:T(8,128)} copy(f32[130,24,1]{2,1,0:T(8,128)} %get-tuple-element.25) | data formatting | bytes 24960 | tf_op jit(solution)/shard_map/slice | solution.py:11
  172.3 3.0 %copy.28 = f32[130,24,1]{0,1,2:T(8,128)} copy(f32[130,24,1]{2,1,0:T(8,128)} %get-tuple-element.26) | data formatting | bytes 24960 | tf_op jit(solution)/shard_map/slice | solution.py:12
  175.3 6.9 %collective-permute-start.3 = (f32[130,24,1]{0,1,2:T(8,128)}, f32[130,24,1]{0,1,2:T(8,128)}, u32[]{:S(2)}, u32[]{:S(2)}) collective-permute-start(f32[130,24,1]{0,1,2:T(8,128)} %copy.28), channel_id=1, source_target_pairs={{0,1},{1,2},{2,3},{3,4},{4,5},{5,6},{6,7},{7,8},{8,9},{9,10},{10,1... | collective-permute-start | bytes 37448 | tf_op jit(solution)/shard_map/ppermute | solution.py:15
  182.2 2.1 %collective-permute-start.2 = (f32[130,24,1]{0,1,2:T(8,128)}, f32[130,24,1]{0,1,2:T(8,128)}, u32[]{:S(2)}, u32[]{:S(2)}) collective-permute-start(f32[130,24,1]{0,1,2:T(8,128)} %copy.26), channel_id=1, source_target_pairs={{1,0},{2,1},{3,2},{4,3},{5,4},{6,5},{7,6},{8,7},{9,8},{10,9},{11,1... | collective-permute-start | bytes 37448 | tf_op jit(solution)/shard_map/ppermute | solution.py:17
  184.3 2.0 pad_maximum_fusion.9
  186.3 5.0 %collective-permute-done.2 = f32[130,24,1]{0,1,2:T(8,128)} collective-permute-done((f32[130,24,1]{0,1,2:T(8,128)}, f32[130,24,1]{0,1,2:T(8,128)}, u32[]{:S(2)}, u32[]{:S(2)}) %collective-permute-start.2) | collective-permute-done | bytes 12512 | tf_op jit(solution)/shard_map/ppermute | solution.py:17
  191.3 2.8 %copy.27 = f32[130,24,1]{2,1,0:T(8,128)} copy(f32[130,24,1]{0,1,2:T(8,128)} %collective-permute-done.2) | data formatting | bytes 24960 | tf_op jit(solution)/shard_map/ppermute | solution.py:17
  194.1 2.8 %copy.29 = f32[130,24,1]{2,1,0:T(8,128)} copy(f32[130,24,1]{0,1,2:T(8,128)} %collective-permute-done.3) | data formatting | bytes 24960 | tf_op jit(solution)/shard_map/ppermute | solution.py:15
  196.9 7.4 %fusion.3 = f32[128,24,256]{2,1,0:T(8,128)} fusion(f32[128,24,256]{2,1,0:T(8,128)S(1)} %bitcast_add_fusion, f32[130,24,1]{2,1,0:T(8,128)} %copy.29, f32[1,24,256]{2,1,0:T(8,128)S(1)} %copy-done.9, f32[1,24,256]{2,1,0:T(8,128)S(1)} %copy-done.7, f32[130,24,1]{2,1,0:T(8,128)} %copy.27, f32[24]{0:T(128)S(1)} %copy-done.12), kind=kLoop, calls=%fused_computation.5 | loop fusion | flops 11796480 | bytes 6365664 | tf_op jit(solution)/shard_map/add | solution.py:87
  (35 shorter events, 0.5 us)
Async XLA Ops:
  0.6 145.7 %copy-start = (f32[24,24]{1,0:T(8,128)S(1)}, f32[24,24]{1,0:T(8,128)}, u32[]{:S(2)}) copy-start(f32[24,24]{1,0:T(8,128)} %param.12) | copy-start | bytes 6916
  0.6 7.0 %copy-start.11 = (s32[8,2]{0,1:T(2,128)S(1)}, s32[8,2]{0,1:T(2,128)}, u32[]{:S(2)}) copy-start(s32[8,2]{0,1:T(2,128)} %param.11) | copy-start | bytes 196
  0.7 12.7 %copy-start.10 = (s32[4,16]{1,0:T(4,128)S(1)}, s32[4,16]{1,0:T(4,128)}, u32[]{:S(2)}) copy-start(s32[4,16]{1,0:T(4,128)} %param.10) | copy-start | bytes 772
  0.7 46.2 %all-to-all-start = ((f32[128,24,256]{2,1,0:T(8,128)}), f32[128,24,256]{2,1,0:T(8,128)S(1)}, u32[]{:S(2)}, u32[]{:S(2)}) async-start(f32[128,24,256]{2,1,0:T(8,128)} %param.8), calls=%async_computation | async-start | bytes 6291456 | tf_op jit(solution)/shard_map/all_to_all | solution.py:54
  98.1 48.2 %all-to-all-start.1 = ((f32[128,24,256]{2,1,0:T(8,128)}), f32[128,24,256]{2,1,0:T(8,128)}, u32[]{:S(2)}, u32[]{:S(2)}) async-start(f32[128,24,256]{2,1,0:T(8,128)} %bitcast_select_fusion), calls=%async_computation.1 | async-start | bytes 6291456 | tf_op jit(solution)/shard_map/all_to_all | solution.py:71
  146.3 15.5 %copy-start.2 = (f32[8,24,256]{2,1,0:T(8,128)S(1)}, f32[8,24,256]{2,1,0:T(8,128)}, u32[]{:S(2)}) copy-start(f32[8,24,256]{2,1,0:T(8,128)} %get-tuple-element.22) | copy-start | bytes 589828
  146.3 15.5 %copy-start.3 = (f32[8,24,256]{2,1,0:T(8,128)S(1)}, f32[8,24,256]{2,1,0:T(8,128)}, u32[]{:S(2)}) copy-start(f32[8,24,256]{2,1,0:T(8,128)} %get-tuple-element.23) | copy-start | bytes 589828
  146.3 15.6 %copy-start.4 = (f32[8,24,256]{2,1,0:T(8,128)S(1)}, f32[8,24,256]{2,1,0:T(8,128)}, u32[]{:S(2)}) copy-start(f32[8,24,256]{2,1,0:T(8,128)} %get-tuple-element.24) | copy-start | bytes 589828
  153.5 13.0 %collective-permute-start.1 = (f32[1,24,256]{2,1,0:T(8,128)S(1)}, f32[1,24,256]{2,1,0:T(8,128)S(1)}, u32[]{:S(2)}, u32[]{:S(2)}) collective-permute-start(f32[1,24,256]{2,1,0:T(8,128)S(1)} %get-tuple-element.27), channel_id=1, source_target_pairs={{0,16},{16,32},{32,48},{48,64},{64,80},{80,96},{96,112},{1,17},{17... | collective-permute-start | bytes 73736 | tf_op jit(solution)/shard_map/ppermute | solution.py:15
  157.0 9.5 %collective-permute-start = (f32[1,24,256]{2,1,0:T(8,128)S(1)}, f32[1,24,256]{2,1,0:T(8,128)S(1)}, u32[]{:S(2)}, u32[]{:S(2)}) collective-permute-start(f32[1,24,256]{2,1,0:T(8,128)S(1)} %get-tuple-element.28), channel_id=1, source_target_pairs={{16,0},{32,16},{48,32},{64,48},{80,64},{96,80},{112,96},{17,1},{33... | collective-permute-start | bytes 73736 | tf_op jit(solution)/shard_map/ppermute | solution.py:17
  166.5 0.6 copy-start.6
  166.5 0.6 copy-start.8
  169.3 15.0 %copy-start.1 = (f32[8,1,24,256]{3,2,1,0:T(8,128)S(1)}, f32[8,1,24,256]{3,2,1,0:T(8,128)}, u32[]{:S(2)}) copy-start(f32[8,1,24,256]{3,2,1,0:T(8,128)} %get-tuple-element.19) | copy-start | bytes 589828
  169.3 15.0 %copy-start.5 = (f32[8,1,24,256]{3,2,1,0:T(8,128)S(1)}, f32[8,1,24,256]{3,2,1,0:T(8,128)}, u32[]{:S(2)}) copy-start(f32[8,1,24,256]{3,2,1,0:T(8,128)} %get-tuple-element.29) | copy-start | bytes 589828
  172.3 24.6 %copy-start.12 = (f32[24]{0:T(128)S(1)}, f32[24]{0:T(128)}, u32[]{:S(2)}) copy-start(f32[24]{0:T(128)} %param.13) | copy-start | bytes 292
  175.3 18.8 %collective-permute-start.3 = (f32[130,24,1]{0,1,2:T(8,128)}, f32[130,24,1]{0,1,2:T(8,128)}, u32[]{:S(2)}, u32[]{:S(2)}) collective-permute-start(f32[130,24,1]{0,1,2:T(8,128)} %copy.28), channel_id=1, source_target_pairs={{0,1},{1,2},{2,3},{3,4},{4,5},{5,6},{6,7},{7,8},{8,9},{9,10},{10,1... | collective-permute-start | bytes 37448 | tf_op jit(solution)/shard_map/ppermute | solution.py:15
  182.2 9.1 %collective-permute-start.2 = (f32[130,24,1]{0,1,2:T(8,128)}, f32[130,24,1]{0,1,2:T(8,128)}, u32[]{:S(2)}, u32[]{:S(2)}) collective-permute-start(f32[130,24,1]{0,1,2:T(8,128)} %copy.26), channel_id=1, source_target_pairs={{1,0},{2,1},{3,2},{4,3},{5,4},{6,5},{7,6},{8,7},{9,8},{10,9},{11,1... | collective-permute-start | bytes 37448 | tf_op jit(solution)/shard_map/ppermute | solution.py:17
  186.3 10.6 %copy-start.7 = (f32[1,24,256]{2,1,0:T(8,128)S(1)}, f32[1,24,256]{2,1,0:T(8,128)}, u32[]{:S(2)}) copy-start(f32[1,24,256]{2,1,0:T(8,128)} %copy-done.6) | copy-start | bytes 73732
  186.3 10.6 %copy-start.9 = (f32[1,24,256]{2,1,0:T(8,128)S(1)}, f32[1,24,256]{2,1,0:T(8,128)}, u32[]{:S(2)}) copy-start(f32[1,24,256]{2,1,0:T(8,128)} %copy-done.8) | copy-start | bytes 73732

commit v2 on v1

v2 whole, which is shorter than its diff:
```python
import jax
import jax.numpy as jnp
from jax import lax
from jax.experimental import pallas as pl
from jax.experimental.pallas import tpu as pltpu
from jax.sharding import PartitionSpec as P

CHUNK_STRIPS = 4
VMEM_BYTES = 40 * 1024 * 1024
SMEM = pl.BlockSpec(memory_space=pltpu.SMEM)
VMEM = pl.BlockSpec(memory_space=pltpu.VMEM)


def coefficients(float_weights, lost_a, lost_b):
    weight_a = jnp.take(float_weights, lost_a, axis=1)
    weight_b = jnp.take(float_weights, lost_b, axis=1)
    gram_aa = jnp.sum(weight_a * weight_a) + 1.0
    gram_bb = jnp.sum(weight_b * weight_b) + 1.0
    gram_ab = jnp.sum(weight_a * weight_b)
    determinant = gram_aa * gram_bb - gram_ab * gram_ab
    coeff_a = (gram_bb * weight_a - gram_ab * weight_b) / determinant
    coeff_b = (gram_aa * weight_b - gram_ab * weight_a) / determinant
    return weight_a, weight_b, coeff_a, coeff_b


def sums_kernel(lost, weights, pair, strips, saved, parity, rebuilt, back, edges):
    count, rows, fields, columns = strips.shape
    checks = saved.shape[1]
    half = columns // 2
    some = rows // 2
    wide = 2 * fields
    part = pl.program_id(0)
    lane = lax.broadcasted_iota(jnp.int32, (fields, half), 1)

    @pl.when(part == 0)
    def _():
        edges[...] = jnp.zeros_like(edges)

    @pl.loop(0, some)
    def _(p):
        i = part * some + p
        at = pl.multiple_of(i * wide, 8)
        to = pl.multiple_of(fields + p * wide, 8)
        living = [None] * checks
        for c in range(count):
            block = strips[c, i]
            for k in range(checks):
                term = weights[k, c] * block
                living[k] = term if c == 0 else living[k] + term
        whole = [jnp.zeros_like(living[0]), jnp.zeros_like(living[0])]
        for k in range(checks):
            residue = saved[p, k] - living[k]
            for b in range(2):
                whole[b] = whole[b] + pair[2 + b, k] * residue
        for k in range(checks):
            parity[p, k] = living[k] + pair[0, k] * whole[0] + pair[1, k] * whole[1]
        lines = []
        for b in range(2):
            lines.append(jnp.concatenate([whole[b][:, :half], whole[b][:, half:]], axis=0))
            rebuilt[b, pl.ds(at, wide), :] = lines[b]
            final = jnp.broadcast_to(whole[b][:, columns - 1 :], (fields, half))
            first = jnp.broadcast_to(whole[b][:, :1], (fields, half))
            kept = jnp.where(lane == i, final, edges[b])
            edges[b] = jnp.where(lane == i + rows, first, kept)
        for c in range(count // 2):
            back[2 * c + part, pl.ds(to, wide), :] = jnp.where(lost[0] // 2 == c, lines[0], lines[1])

    @pl.when(part == 1)
    def _():
        for c in range(count):
            west = jnp.where(lost[0] == c - 1, edges[0], edges[1])
            east = jnp.where(lost[0] == c + 1, edges[0], edges[1])
            back[c, 0:fields, :] = jnp.where(lane < rows, west, east)


def sums(lost, weights, pair, strips, saved):
    count, rows, fields, columns = strips.shape
    checks = saved.shape[1]
    half = columns // 2
    rows_of = pl.BlockSpec((rows // 2, checks, fields, columns), lambda g: (g, 0, 0, 0))
    return pl.pallas_call(
        sums_kernel,
        grid=(2,),
        out_shape=(
            jax.ShapeDtypeStruct(saved.shape, jnp.float32),
            jax.ShapeDtypeStruct((2, 2 * rows * fields, half), jnp.float32),
            jax.ShapeDtypeStruct((count, (rows + 1) * fields, half), jnp.float32),
        ),
        in_specs=[SMEM, SMEM, SMEM, VMEM, rows_of],
        out_specs=(rows_of, VMEM, VMEM),
        scratch_shapes=[pltpu.VMEM((2, fields, half), jnp.float32)],
        compiler_params=pltpu.CompilerParams(
            vmem_limit_bytes=VMEM_BYTES, dimension_semantics=("arbitrary",)
        ),
        cost_estimate=pl.CostEstimate(
            flops=8 * strips.size, bytes_accessed=8 * strips.size, transcendentals=0
        ),
    )(lost, weights, pair, strips, saved)


def spread_kernel(lost, rebuilt, short, back):
    count = short.shape[0]
    fields = back.shape[1] - rebuilt.shape[1]
    for c in range(count):
        back[c, 0:fields, :] = short[c, 0:fields, :]
        back[c, fields:, :] = jnp.where(lost[0] == c, rebuilt[0], rebuilt[1])


def spread_whole(lost, rebuilt, short):
    count, lines, half = short.shape
    whole = rebuilt.shape[1]
    fields = lines - whole // 2
    return pl.pallas_call(
        spread_kernel,
        out_shape=jax.ShapeDtypeStruct((count, fields + whole, half), jnp.float32),
        in_specs=[SMEM, VMEM, VMEM],
        out_specs=VMEM,
        compiler_params=pltpu.CompilerParams(vmem_limit_bytes=VMEM_BYTES),
    )(lost, rebuilt, short)


def step_kernel(
    flags, ocean, mine, other, op, number_of, west_raw, east_raw, out, mixed, sides, operator
):
    rows, fields, columns = ocean.shape
    half = columns // 2
    wide = 2 * fields
    count = mine.shape[0]
    strip = rows // count
    step = pl.program_id(0)
    lost = flags[0] != 0
    mine_first = flags[1] == 0
    lane = lax.broadcasted_iota(jnp.int32, (fields, half), 1)
    number = number_of[...]

    def mix_pair(flat):
        high = flat.astype(jnp.bfloat16)
        low = (flat - high.astype(jnp.float32)).astype(jnp.bfloat16)
        terms = jnp.concatenate([high, low, high], axis=0)
        return flat + jnp.tanh(
            jnp.dot(operator[...], terms, preferred_element_type=jnp.float32)
        )

    def mix(s):
        base = pl.multiple_of(s * strip, strip)
        head = None
        for t in range(0, strip, 2):
            units = []
            for q in (t, t + 1):
                p = fields + (q % (strip // 2)) * wide
                use_mine = mine_first if q < strip // 2 else jnp.logical_not(mine_first)
                sent = jnp.where(use_mine, mine[s, p : p + wide, :], other[s, p : p + wide, :])
                sent = jnp.concatenate([sent[:fields], sent[fields:]], axis=1)
                units.append(jnp.where(lost, sent, ocean[base + q]))
            done = mix_pair(jnp.concatenate(units, axis=0)).reshape(2, fields, columns)
            mixed[pl.ds(base + t + 1, 2)] = done
            if t == 0:
                head = done[0]
        return head

    @pl.when(step == 0)
    def _():
        both = op[...]
        high = both.astype(jnp.bfloat16)
        low = (both - high.astype(jnp.float32)).astype(jnp.bfloat16)
        operator[...] = jnp.concatenate([high, high, low], axis=1)
        mixed[0] = jnp.zeros((fields, columns), jnp.float32)
        mixed[rows + 1] = jnp.zeros((fields, columns), jnp.float32)
        west = jnp.zeros((fields, half), jnp.float32)
        east = jnp.zeros((fields, half), jnp.float32)
        for s in range(count):
            sent = mine[s, 0:fields, :]
            here = (lane >= s * strip) & (lane < (s + 1) * strip)
            west = jnp.where(here, pltpu.roll(sent, s * strip, 1) if s else sent, west)
            east = jnp.where(here, pltpu.roll(sent, (s * strip - strip) % half, 1) if s != 1 else sent, east)
        west = jnp.where(flags[2] != 0, west, west_raw[...])
        east = jnp.where(flags[3] != 0, east, east_raw[...])
        both_sides = jnp.concatenate([west, east], axis=1)
        both_sides = mix_pair(jnp.concatenate([both_sides, both_sides], axis=0))
        sides[0] = both_sides[:fields, :half]
        sides[1] = pltpu.roll(both_sides[:fields, half:], half - 1, 1)
        mix(0)

    def diffuse(s, t, below, west_side, east_side):
        i = s * strip + t + 1
        for part in range(2):
            own = slice(part * half, (part + 1) * half)
            here = mixed[i, :, own]
            across = mixed[i, :, (1 - part) * half : (2 - part) * half]
            if part == 0:
                side = pltpu.roll(west_side, half - t, 1) if t else west_side
                west = jnp.where(lane == 0, side, pltpu.roll(here, 1, 1))
                east = pltpu.roll(jnp.where(lane == 0, across, here), half - 1, 1)
            else:
                side = pltpu.roll(east_side, half - t, 1) if t else east_side
                west = pltpu.roll(jnp.where(lane == half - 1, across, here), 1, 1)
                east = jnp.where(lane == half - 1, side, pltpu.roll(here, half - 1, 1))
            under = mixed[i + 1, :, own] if below is None else below[:, own]
            around = under + mixed[i - 1, :, own] + east + west
            out[(s - step * CHUNK_STRIPS) * strip + t, :, own] = here + number * (
                around - 4.0 * here
            )

    def body(j, carry):
        s = step * CHUNK_STRIPS + j
        for t in range(strip - 1):
            diffuse(s, t, None, *carry)
        head = mix(jnp.minimum(s + 1, count - 1))
        head = jnp.where(s == count - 1, mixed[rows + 1], head)
        diffuse(s, strip - 1, head, *carry)
        return pltpu.roll(carry[0], half - strip, 1), pltpu.roll(carry[1], half - strip, 1)

    west_side, east_side = lax.fori_loop(0, CHUNK_STRIPS, body, (sides[0], sides[1]))
    sides[0] = west_side
    sides[1] = east_side


def step(flags, ocean, mine, other, op, number_of, west_raw, east_raw):
    rows, fields, columns = ocean.shape
    chunk = CHUNK_STRIPS * rows // mine.shape[0]
    return pl.pallas_call(
        step_kernel,
        grid=(rows // chunk,),
        out_shape=jax.ShapeDtypeStruct(ocean.shape, jnp.float32),
        in_specs=[SMEM] + [VMEM] * 7,
        out_specs=pl.BlockSpec((chunk, fields, columns), lambda g: (g, 0, 0)),
        scratch_shapes=[
            pltpu.VMEM((rows + 2, fields, columns), jnp.float32),
            pltpu.VMEM((2, fields, columns // 2), jnp.float32),
            pltpu.VMEM((2 * fields, 6 * fields), jnp.bfloat16),
        ],
        compiler_params=pltpu.CompilerParams(
            vmem_limit_bytes=VMEM_BYTES, dimension_semantics=("arbitrary",)
        ),
        cost_estimate=pl.CostEstimate(
            flops=150 * ocean.size, bytes_accessed=12 * ocean.size, transcendentals=ocean.size
        ),
    )(flags, ocean, mine, other, op, number_of, west_raw, east_raw)


def ends_kernel(stepped, above, below, op, number_of, out, row, sem):
    rows, fields, columns = stepped.shape
    outer = ((0, above), (rows - 1, below))
    reads = [
        pltpu.make_async_copy(out.at[at], row.at[n], sem.at[n]) for n, (at, _) in enumerate(outer)
    ]
    for copy in reads:
        copy.start()
    both = jnp.concatenate([above[...], below[...]], axis=0)
    coupled = jnp.dot(
        op[...], both, preferred_element_type=jnp.float32, precision=lax.Precision.HIGHEST
    )
    both = both + jnp.tanh(coupled)
    number = jnp.concatenate([number_of[...], number_of[...]], axis=1)
    writes = []
    for n, (at, _) in enumerate(outer):
        reads[n].wait()
        row[n] = row[n] + number * both[n * fields : (n + 1) * fields]
        writes.append(pltpu.make_async_copy(row.at[n], out.at[at], sem.at[n]))
        writes[n].start()
    for copy in writes:
        copy.wait()


def add_ends(stepped, above, below, op, number_of):
    fields, columns = above.shape
    anywhere = pl.BlockSpec(memory_space=pl.ANY)
    return pl.pallas_call(
        ends_kernel,
        out_shape=jax.ShapeDtypeStruct(stepped.shape, jnp.float32),
        in_specs=[anywhere] + [VMEM] * 4,
        out_specs=anywhere,
        input_output_aliases={0: 0},
        scratch_shapes=[
            pltpu.VMEM((2, fields, columns), jnp.float32),
            pltpu.SemaphoreType.DMA((2,)),
        ],
        compiler_params=pltpu.CompilerParams(vmem_limit_bytes=VMEM_BYTES),
    )(stepped, above, below, op, number_of)


def per_device(
    ocean_state, saved_checksums, checksum_weights, failed_devices, column_op, diffusivity
):
    count = lax.axis_size("col")
    lines = lax.axis_size("row")
    my_col = lax.axis_index("col")
    my_row = lax.axis_index("row")
    rows, fields, columns = ocean_state.shape
    half = columns // 2
    strip = rows // count
    east_pairs = [(i, i + 1) for i in range(count - 1)]
    west_pairs = [(i + 1, i) for i in range(count - 1)]
    down_pairs = [(i, i + 1) for i in range(lines - 1)]
    up_pairs = [(i + 1, i) for i in range(lines - 1)]
    twin_pairs = [(i, i ^ 1) for i in range(count)]

    strips = lax.all_to_all(ocean_state, "col", 0, 0, tiled=True)
    strips = strips.reshape(count, strip, fields, columns)

    west_raw = lax.ppermute(ocean_state[:, :, columns - 1].T, "col", east_pairs)
    east_raw = lax.ppermute(ocean_state[:, :, 0].T, "col", west_pairs)

    lost_pair = lax.dynamic_index_in_dim(failed_devices, my_row, 0, keepdims=False)
    lost_a = lost_pair[0]
    lost_b = lost_pair[1]
    same_chip = jnp.any(failed_devices[:, 0] // 2 == failed_devices[:, 1] // 2)
    float_weights = checksum_weights.astype(jnp.float32)
    pair = jnp.stack(coefficients(float_weights, lost_a, lost_b))
    members = jnp.arange(count)
    survive_weights = jnp.where((members == lost_a) | (members == lost_b), 0.0, float_weights)

    def is_lost(member):
        return (member == lost_a) | (member == lost_b)

    flags = jnp.stack(
        [
            is_lost(my_col),
            (my_col % 2 == 1) & ~same_chip,
            is_lost(my_col - 1),
            is_lost(my_col + 1),
        ]
    ).astype(jnp.int32)
    op = jnp.kron(jnp.eye(2, dtype=jnp.float32), column_op)
    number_of = jnp.broadcast_to(diffusivity[:, None], (fields, half))

    fresh_parity, rebuilt, back = sums(
        lost_pair, survive_weights, pair, strips, saved_checksums
    )

    def exchange_halves(rebuilt, back):
        mine = lax.all_to_all(back, "col", 0, 0, tiled=True)
        return mine, lax.ppermute(mine, "col", twin_pairs)

    def exchange_whole(rebuilt, back):
        got = lax.all_to_all(spread_whole(lost_pair, rebuilt, back), "col", 0, 0, tiled=True)
        length = back.shape[1]
        return got[:, :length], got[:, length - fields :]

    mine, other = lax.cond(same_chip, exchange_whole, exchange_halves, rebuilt, back)

    mine_first = flags[1] == 0
    lost = flags[0] != 0

    def sent_row(first, at):
        sent = jnp.where(first, mine[at], other[at])
        return sent

    top = jnp.where(mine_first, mine[0, fields : 3 * fields], other[0, fields : 3 * fields])
    bottom = jnp.where(mine_first, other[count - 1, -2 * fields :], mine[count - 1, -2 * fields :])
    top = jnp.concatenate([top[:fields], top[fields:]], axis=1)
    bottom = jnp.concatenate([bottom[:fields], bottom[fields:]], axis=1)
    top = jnp.where(lost, top, ocean_state[0])
    bottom = jnp.where(lost, bottom, ocean_state[rows - 1])
    above = lax.ppermute(bottom, "row", down_pairs)
    below = lax.ppermute(top, "row", up_pairs)
    stepped_state = step(
        flags, ocean_state, mine, other, op, number_of, west_raw, east_raw
    )
    stepped_state = add_ends(stepped_state, above, below, op, number_of)
    return (stepped_state, fresh_parity)


def solution(mesh):
    return jax.shard_map(
        per_device,
        mesh=mesh,
        in_specs=(P("row", None, "col"), P(("row", "col"), None, None, None), P(), P(), P(), P()),
        out_specs=(P("row", None, "col"), P(("row", "col"), None, None, None)),
        check_vma=False,
    )
```

time: 206 us -> 124 us (0.60)
  other arithmetic: 68.2 us -> 3.74 us
  waiting for transfers between devices: 68 us -> 8.65 us
  blocking collectives: 0 us -> 49.5 us
  Pallas kernels: 0 us -> 15 us
  starting transfers between devices: 33.4 us -> 22.3 us
  local copies, waits for them, and re-layouts: 19.3 us -> 8.86 us
  matrix products: 7.12 us -> 0 us
  between operations: 8.32 us -> 13.6 us
    another operation x3 -> x2, other arithmetic: 55.8 us -> 0.64 us  [per_device(): pair = jnp.stack(coefficients(float_weights, lost_a, lost_b))]
    all_to_all x0 -> x1, blocking collectives: none -> 49.5 us  [exchange_whole(): lax.all_to_all(spread_whole(lost_pair, rebuilt, back), 'col', 0, 0, tiled...]
    all_to_all x1 -> x0, waiting for transfers between devices: 38 us -> none  [per_device(): lax.all_to_all(back.reshape(rows, fields, columns), 'col', 0, 0, tiled=True)]
    all_to_all x1, waiting for transfers between devices: 25.1 us -> 8.64 us  [per_device(): strips = lax.all_to_all(ocean_state, 'col', 0, 0, tiled=True)]
    pallas_call x0 -> x4, Pallas kernels: none -> 15 us  [the longest x1 8.28 us: step(): pl.pallas_call(step_kernel, grid=(rows // chunk,), out_shape=jax.ShapeDty...]
    slice x11 -> x5, local copies, waits for them, and re-layouts: 13 us -> 3.56 us  [the longest x1 2.16 us: per_device(): east_raw = lax.ppermute(ocean_state[:, :, 0].T, 'col', west_pairs)]
    all_to_all x1 -> x0, starting transfers between devices: 9.02 us -> none  [per_device(): lax.all_to_all(back.reshape(rows, fields, columns), 'col', 0, 0, tiled=True)]
    add x1 -> x0, other arithmetic: 7.4 us -> none  [per_device(): stepped_state = mixed_state + diffusivity[None, :, None] * laplace_term]
  transfers between devices with their start and end apart: 6 -> 5, of which waited for: 3 -> 1; matrix products, arithmetic and copies ran while one was open for 8% -> 9% of each run, Pallas kernels for 0% -> 11%
where the time goes in v2:
time: 124 us; the launch traced here: 122 us
  blocking collectives  49.5 us (40%)
  starting transfers between devices  22.3 us (18%)
  Pallas kernels  15 us (12%)
  between operations  13.6 us (11%)
  local copies, waits for them, and re-layouts  8.86 us (7%)
  waiting for transfers between devices  8.65 us (7%)
  other arithmetic  3.74 us (3%)
    all_to_all x1, blocking collectives, exchange_whole(): lax.all_to_all(spread_whole(lost_pair, rebuilt, back), 'col', 0, 0, tiled...  49.5 us
    all_to_all x1, waiting for transfers between devices, per_device(): strips = lax.all_to_all(ocean_state, 'col', 0, 0, tiled=True)  8.64 us
    pallas_call x1, Pallas kernels, step(): pl.pallas_call(step_kernel, grid=(rows // chunk,), out_shape=jax.ShapeDty...  8.28 us
    all_to_all x1, starting transfers between devices, per_device(): strips = lax.all_to_all(ocean_state, 'col', 0, 0, tiled=True)  7.11 us
    unnamed x18, local copies, waits for them, and re-layouts  4.95 us
    ppermute x1, starting transfers between devices, per_device(): west_raw = lax.ppermute(ocean_state[:, :, columns - 1].T, 'col', east_pairs)  4.84 us
    ppermute x1, starting transfers between devices, per_device(): below = lax.ppermute(top, 'row', up_pairs)  4.83 us
    pallas_call x1, Pallas kernels, sums(): pl.pallas_call(sums_kernel, grid=(2,), out_shape=(jax.ShapeDtypeStruct(sa...  4.49 us
  transfers between devices with their start and end apart: 5, of which 1 were waited for; matrix products, arithmetic and copies ran while one was open for 9% of the time, Pallas kernels for 11%

profile of v2, /device:TPU:15, one launch (start us, length us, event | category | flops | bytes accessed | tf_op | source)
XLA Modules:
  0.0 121.6 jit_solution(7182181351984364200)
XLA Ops:
  0.6 7.1 %all-to-all-start.2 = ((f32[128,24,256]{2,1,0:T(8,128)}), f32[128,24,256]{2,1,0:T(8,128)}, u32[]{:S(2)}, u32[]{:S(2)}) async-start(f32[128,24,256]{2,1,0:T(8,128)} %ocean.1), calls=%async_computation.2 | async-start | bytes 6291456 | tf_op jit(solution)/shard_map/all_to_all | solution.py:298
  7.8 2.2 %fusion.2 = (f32[128,24,1]{2,1,0:T(8,128)}, f32[128,24,1]{2,1,0:T(8,128)}) fusion(f32[128,24,256]{2,1,0:T(8,128)S(1)} %copy-done), kind=kLoop, calls=%fused_computation.35 | loop fusion | bytes 49152 | tf_op jit(solution)/shard_map/slice | solution.py:302
  9.9 1.9 %copy.13 = f32[128,24,1]{0,1,2:T(8,128)S(1)} copy(f32[128,24,1]{2,1,0:T(8,128)} %get-tuple-element.48) | data formatting | bytes 24576
  11.8 4.8 %collective-permute-start.1 = (f32[24,128]{1,0:T(8,128)S(1)}, f32[24,128]{1,0:T(8,128)S(1)}, u32[]{:S(2)}, u32[]{:S(2)}) collective-permute-start(f32[24,128]{1,0:T(8,128)S(1)} %bitcast.53), channel_id=1, source_target_pairs={{0,1},{1,2},{2,3},{3,4},{4,5},{5,6},{6,7},{7,8},{8,9},{9,10},{10,1... | collective-permute-start | bytes 36872 | tf_op jit(solution)/shard_map/ppermute | solution.py:301
  16.7 1.9 %copy.14 = f32[128,24,1]{0,1,2:T(8,128)S(1)} copy(f32[128,24,1]{2,1,0:T(8,128)} %get-tuple-element.47) | data formatting | bytes 24576
  18.6 1.9 %collective-permute-start.2 = (f32[24,128]{1,0:T(8,128)S(1)}, f32[24,128]{1,0:T(8,128)S(1)}, u32[]{:S(2)}, u32[]{:S(2)}) collective-permute-start(f32[24,128]{1,0:T(8,128)S(1)} %bitcast.54), channel_id=1, source_target_pairs={{1,0},{2,1},{3,2},{4,3},{5,4},{6,5},{7,6},{8,7},{9,8},{10,9},{11,1... | collective-permute-start | bytes 36872 | tf_op jit(solution)/shard_map/ppermute | solution.py:302
  20.5 0.2 fusion
  20.7 0.5 fusion.3
  25.1 0.7 compare_reduce_fusion
  31.0 0.2 select_reduce_fusion
  31.2 0.7 multiply_reduce_fusion.1
  34.4 0.1 add_convert_fusion.flags
  34.4 0.7 fusion.4
  36.3 1.3 %compare_or_fusion = pred[16]{0:T(512)(128)(4,1)S(1)} fusion(s32[]{:T(128)} %bitcast.1, s32[]{:T(128)} %bitcast), kind=kLoop, calls=%fused_computation.14 | loop fusion | flops 48 | bytes 24 | tf_op jit(solution)/shard_map/or | solution.py:311
  37.6 0.6 divide_bitcast_fusion.1
  38.3 8.6 %all-to-all-done.2 = f32[128,24,256]{2,1,0:T(8,128)} async-done(((f32[128,24,256]{2,1,0:T(8,128)}), f32[128,24,256]{2,1,0:T(8,128)}, u32[]{:S(2)}, u32[]{:S(2)}) %all-to-all-start.2) | async-done | bytes 3145760 | tf_op jit(solution)/shard_map/all_to_all | solution.py:298
  46.9 1.1 copy-done.1
  48.1 4.5 %shard_map.77 = (f32[8,4,24,256]{3,2,1,0:T(8,128)}, f32[2,384,128]{2,1,0:T(8,128)S(1)}, f32[16,216,128]{2,1,0:T(8,128)S(1)}) custom-call(s32[2]{0:T(128)S(1)} %get-tuple-element.39.lost, f32[4,16]{1,0:T(4,128)S(1)} %broadcast_select_fusion.weights, f32[4,4]{1,0:T(4,128)S(1)} %pad_maximum_fusion.pair, f32[16,8,24,256]{3,2,1,0:T(8,128)} %bitcast.10.strips, ...), custom_call_target="tpu_custom_call" | custom-call | flops 6291456 | bytes 6291456 | tf_op jit(solution)/shard_map/pallas_call | solution.py:81
  52.6 50.5 %conditional.1 = (f32[16,216,128]{2,1,0:T(8,128)S(1)}, f32[16,216,128]{2,1,0:T(8,128)S(1)}) conditional(s32[]{:T(128)} %convert_element_type.17, f32[16,216,128]{2,1,0:T(8,128)S(1)} %get-tuple-element.18, (s32[2]{0:T(128)S(1)}, f32[2,384,128]{2,1,0:T(8,128)S(1)}, f32[16,216,128]{2,1,0:T(8,128)S(1)}) %tuple.17), branch_computations={%region_4.6_spmd, %region_5.7_spmd} | conditional | bytes 13762576 | solution.py:340
  52.6 0.8 branch_1_fun.1
  53.4 49.5 %all_to_all.14 = f32[16,408,128]{2,1,0:T(8,128)S(1)} all-to-all(f32[16,408,128]{2,1,0:T(8,128)S(1)} %branch_1_fun.1), channel_id=1, replica_groups=mesh['row'=8,'col'=16] {'col'}, dimensions={0} | all-to-all | bytes 6684672 | tf_op jit(solution)/shard_map/cond/branch_1_fun/all_to_all | solution.py:336
  102.9 0.2 fusion.1
  103.2 3.5 %collective-permute-start.3 = (f32[24,256]{1,0:T(8,128)S(1)}, f32[24,256]{1,0:T(8,128)S(1)}, u32[]{:S(2)}, u32[]{:S(2)}) collective-permute-start(f32[24,256]{1,0:T(8,128)S(1)} %get-tuple-element.46), channel_id=1, source_target_pairs={{0,16},{16,32},{32,48},{48,64},{64,80},{80,96},{96,112},{1,17},{17... | collective-permute-start | bytes 73736 | tf_op jit(solution)/shard_map/ppermute | solution.py:355
  106.7 4.8 %collective-permute-start.4 = (f32[24,256]{1,0:T(8,128)S(1)}, f32[24,256]{1,0:T(8,128)S(1)}, u32[]{:S(2)}, u32[]{:S(2)}) collective-permute-start(f32[24,256]{1,0:T(8,128)S(1)} %get-tuple-element.45), channel_id=1, source_target_pairs={{16,0},{32,16},{48,32},{64,48},{80,64},{96,80},{112,96},{17,1},{33... | collective-permute-start | bytes 73736 | tf_op jit(solution)/shard_map/ppermute | solution.py:356
  111.6 0.1 broadcast_multiply_fusion
  111.7 0.1 mul.76.op
  111.8 0.0 collective-permute-done.1.west_raw
  111.8 0.0 collective-permute-done.2.east_raw
  111.8 0.1 broadcast_in_dim.26.number_of
  111.9 8.3 %shard_map.78.stepped = f32[128,24,256]{2,1,0:T(8,128)} custom-call(s32[4]{0:T(128)S(1)} %add_convert_fusion.flags, f32[128,24,256]{2,1,0:T(8,128)S(1)} %copy-done, f32[16,216,128]{2,1,0:T(8,128)} %copy-done.2, f32[16,216,128]{2,1,0:T(8,128)} %copy-done.3, f32[48,48]{1,0:T(8,128)S(1)} %mul.76.op, f32[24,128]{1,0:T(8,128)S(1)} %broadcast_in_dim.26.number_of, ...), custom_call_target="tpu_custom_call" | custom-call | flops 117964800 | bytes 9437184 | tf_op jit(solution)/shard_map/pallas_call | solution.py:221
  120.2 0.0 collective-permute-done.3.above
  120.2 1.4 %shard_map.79 = f32[128,24,256]{2,1,0:T(8,128)} custom-call(f32[128,24,256]{2,1,0:T(8,128)} %shard_map.78.stepped, f32[24,256]{1,0:T(8,128)S(1)} %collective-permute-done.3.above, f32[24,256]{1,0:T(8,128)S(1)} %collective-permute-done.4.below, f32[48,48]{1,0:T(8,128)S(1)} %mul.76.op, ...), custom_call_target="tpu_custom_call", output_to_operand_aliasing={{}: (0, {})} | custom-call | tf_op jit(solution)/shard_map/pallas_call | solution.py:268
  (23 shorter events, 0.1 us)
Async XLA Ops:
  0.6 7.1 %copy-start = (f32[128,24,256]{2,1,0:T(8,128)S(1)}, f32[128,24,256]{2,1,0:T(8,128)}, u32[]{:S(2)}) copy-start(f32[128,24,256]{2,1,0:T(8,128)} %ocean.1) | copy-start | bytes 9437188
  0.6 46.3 %all-to-all-start.2 = ((f32[128,24,256]{2,1,0:T(8,128)}), f32[128,24,256]{2,1,0:T(8,128)}, u32[]{:S(2)}, u32[]{:S(2)}) async-start(f32[128,24,256]{2,1,0:T(8,128)} %ocean.1), calls=%async_computation.2 | async-start | bytes 6291456 | tf_op jit(solution)/shard_map/all_to_all | solution.py:298
  9.9 10.6 %copy-start.6 = (s32[8,2]{0,1:T(2,128)S(1)}, s32[8,2]{0,1:T(2,128)}, u32[]{:S(2)}) copy-start(s32[8,2]{0,1:T(2,128)} %param.13) | copy-start | bytes 196
  9.9 21.1 %copy-start.5 = (s32[4,16]{1,0:T(4,128)S(1)}, s32[4,16]{1,0:T(4,128)}, u32[]{:S(2)}) copy-start(s32[4,16]{1,0:T(4,128)} %param.12) | copy-start | bytes 772
  11.8 100.0 %collective-permute-start.1 = (f32[24,128]{1,0:T(8,128)S(1)}, f32[24,128]{1,0:T(8,128)S(1)}, u32[]{:S(2)}, u32[]{:S(2)}) collective-permute-start(f32[24,128]{1,0:T(8,128)S(1)} %bitcast.53), channel_id=1, source_target_pairs={{0,1},{1,2},{2,3},{3,4},{4,5},{5,6},{6,7},{7,8},{8,9},{9,10},{10,1... | collective-permute-start | bytes 36872 | tf_op jit(solution)/shard_map/ppermute | solution.py:301
  18.6 93.2 %collective-permute-start.2 = (f32[24,128]{1,0:T(8,128)S(1)}, f32[24,128]{1,0:T(8,128)S(1)}, u32[]{:S(2)}, u32[]{:S(2)}) collective-permute-start(f32[24,128]{1,0:T(8,128)S(1)} %bitcast.54), channel_id=1, source_target_pairs={{1,0},{2,1},{3,2},{4,3},{5,4},{6,5},{7,6},{8,7},{9,8},{10,9},{11,1... | collective-permute-start | bytes 36872 | tf_op jit(solution)/shard_map/ppermute | solution.py:302
  46.9 1.1 copy-start.1
  52.6 59.0 %copy-start.4 = (f32[24,24]{1,0:T(8,128)S(1)}, f32[24,24]{1,0:T(8,128)}, u32[]{:S(2)}) copy-start(f32[24,24]{1,0:T(8,128)} %param.14) | copy-start | bytes 6916
  52.6 59.2 %copy-start.7 = (f32[24]{0:T(128)S(1)}, f32[24]{0:T(128)}, u32[]{:S(2)}) copy-start(f32[24]{0:T(128)} %param.15) | copy-start | bytes 292
  103.1 8.5 %copy-start.2 = (f32[16,216,128]{2,1,0:T(8,128)}, f32[16,216,128]{2,1,0:T(8,128)S(1)}, u32[]{:S(2)}) copy-start(f32[16,216,128]{2,1,0:T(8,128)S(1)} %get-tuple-element.20.mine) | copy-start | bytes 5308420
  103.1 8.5 %copy-start.3 = (f32[16,216,128]{2,1,0:T(8,128)}, f32[16,216,128]{2,1,0:T(8,128)S(1)}, u32[]{:S(2)}) copy-start(f32[16,216,128]{2,1,0:T(8,128)S(1)} %get-tuple-element.21.other) | copy-start | bytes 5308420
  103.2 17.0 %collective-permute-start.3 = (f32[24,256]{1,0:T(8,128)S(1)}, f32[24,256]{1,0:T(8,128)S(1)}, u32[]{:S(2)}, u32[]{:S(2)}) collective-permute-start(f32[24,256]{1,0:T(8,128)S(1)} %get-tuple-element.46), channel_id=1, source_target_pairs={{0,16},{16,32},{32,48},{48,64},{64,80},{80,96},{96,112},{1,17},{17... | collective-permute-start | bytes 73736 | tf_op jit(solution)/shard_map/ppermute | solution.py:355
  106.7 13.4 %collective-permute-start.4 = (f32[24,256]{1,0:T(8,128)S(1)}, f32[24,256]{1,0:T(8,128)S(1)}, u32[]{:S(2)}, u32[]{:S(2)}) collective-permute-start(f32[24,256]{1,0:T(8,128)S(1)} %get-tuple-element.45), channel_id=1, source_target_pairs={{16,0},{32,16},{48,32},{64,48},{80,64},{96,80},{112,96},{17,1},{33... | collective-permute-start | bytes 73736 | tf_op jit(solution)/shard_map/ppermute | solution.py:356
